TPU v7x, 32 devices: a whole 2x2x4 slice. The times are simulated.
32 devices in a mesh: energy: 8 (over y, x, core), mom: 4 (over z).
Axes of the slice: x: 2, y: 2, z: 4, core: 2. Of those that a mesh axis runs over, the one named last changes fastest.
Arguments:
- green: bfloat16 [4, 8, 4, 2, 128, 128], P('mom', 'energy'), may hold values from -6 to 6
- grad: bfloat16 [4, 4, 2, 2, 128, 128], P('mom'), may hold values from -0.375 to 0.375
- coupling: float32 [4, 4], replicated, may hold values from 0.05 to 0.3
- occupation: float32 [4], replicated, may hold values from 0.1 to 2
- offsets: int32 [4], replicated, may hold values from 1 to 4, as said below
- neighbours: int32 [4, 2], replicated, may hold values from 0 to 3
- qtable: int32 [4, 4], P('mom'), may hold values from 0 to 3
Outputs:
- sigma: float32 [4, 8, 4, 2, 128, 128], P('mom', 'energy')
Inputs may be any that keep to these rules, and one draw needn't show every extreme that they name: `offsets`: some mode has offset 1 and some mode has offset 4.
All inputs are finite; a program needn't handle non-finite values.
Results may differ from a plain program's by a relative error of at most 0.0029.
Values may be sent and summed in bfloat16 or wider, within the bound.
A program may use at most 64 MiB of HBM per device.

v0:
```python
import jax
import jax.numpy as jnp
from jax import lax
from jax.sharding import PartitionSpec as P

MAXOFF = 4


def passed_along(value, axis, steps):
    count = lax.axis_size(axis)
    initial, last = (max(0, -steps), min(count, count - steps))
    return lax.ppermute(value, axis, [(source, source + steps) for source in range(initial, last)])


def shards(green, grad, coupling, occupation, offsets, neighbours, qtable):
    clusters = grad.shape[1]
    momenta = coupling.shape[0]
    orbits = grad.shape[4]
    high = lax.Precision.HIGHEST
    pick = (neighbours[:, :, None] == jnp.arange(clusters, dtype=jnp.int32)[None, None, :]).astype(
        jnp.bfloat16
    )
    grad_re = grad[:, :, :, 0]
    grad_im = grad[:, :, :, 1]
    left_block = jnp.concatenate(
        [
            jnp.concatenate([grad_re, -grad_im], axis=-1),
            jnp.concatenate([grad_im, grad_re], axis=-1),
        ],
        axis=-2,
    )
    trans_re = jnp.swapaxes(grad_re, -1, -2)
    trans_im = jnp.swapaxes(grad_im, -1, -2)
    right_block = jnp.concatenate(
        [
            jnp.concatenate([trans_re, -trans_im], axis=-1),
            jnp.concatenate([trans_im, trans_re], axis=-1),
        ],
        axis=-2,
    )
    piece = lax.all_gather(green, "mom", axis=0, tiled=True)
    count = piece.shape[0]
    chosen = jnp.einsum(
        "csx,jxrab->jcsrab", pick, piece[:, 0], preferred_element_type=jnp.float32
    ).astype(jnp.bfloat16)
    chosen = chosen.reshape(count, clusters, chosen.shape[2], 2 * orbits, orbits)
    matches = (qtable[:, :, None] == jnp.arange(momenta, dtype=jnp.int32)[None, None, :]).astype(
        jnp.float32
    )
    weights = jnp.einsum("kjq,qn->kjn", matches, coupling, precision=high)
    product = jnp.einsum(
        "kcsxy,jcsyd->kjcsxd", left_block, chosen, preferred_element_type=jnp.float32
    ).astype(jnp.bfloat16)
    shape = product.shape
    product = product.reshape(shape[0], shape[1], shape[2], shape[3], 2, orbits, orbits)
    product = jnp.swapaxes(product, 4, 5).reshape(
        shape[0], shape[1], shape[2], shape[3], orbits, 2 * orbits
    )
    triple = jnp.einsum(
        "kjcsay,kcsyz->kjcsaz", product, right_block, preferred_element_type=jnp.float32
    )
    triple = triple.reshape(shape[0], shape[1], shape[2], shape[3], orbits, 2, orbits)
    accum = jnp.einsum("kjn,kjcsare->kncrae", weights, triple, precision=high)
    levels = jnp.arange(1, MAXOFF + 1, dtype=jnp.int32)
    select = (offsets[None, :] == levels[:, None]).astype(jnp.float32)
    emitted = jnp.einsum(
        "dn,kncrab->dkcrab", select * (1.0 + occupation[None, :]), accum, precision=high
    )
    absorbed = jnp.einsum("dn,kncrab->dkcrab", select * occupation[None, :], accum, precision=high)
    total = jnp.zeros(emitted.shape[1:], jnp.float32)
    for distance in range(1, MAXOFF + 1):
        total = total + passed_along(emitted[distance - 1], "energy", distance)
        total = total + passed_along(absorbed[distance - 1], "energy", -distance)
    return total[:, None]


def solution(mesh):
    in_specs = (
        P("mom", "energy", None, None, None, None),
        P("mom", None, None, None, None, None),
        P(),
        P(),
        P(),
        P(),
        P("mom", None),
    )
    out_specs = P("mom", "energy", None, None, None, None)
    return jax.shard_map(shards, mesh=mesh, in_specs=in_specs, out_specs=out_specs, check_vma=False)
```

profile of v0, /device:TPU:3, one launch (start us, length us, event | category | flops | bytes accessed | tf_op | source)
XLA Modules:
  0.0 138.8 jit_solution(52025185637781849)
XLA Ops:
  6.5 0.0 copy-start
  6.5 0.0 copy-start.1
  6.5 0.0 all-gather.2.cloned.1.call-start
  6.5 0.7 all-gather.2.cloned.1.call-update
  7.3 0.0 copy-done
  7.3 0.8 convolution_bitcast_fusion.1
  8.1 0.7 broadcast_add_fusion
  8.8 1.0 fusion.43
  9.8 1.0 fusion.44
  10.8 1.3 slice_bitcast_fusion
  12.1 25.9 %all-gather.2.cloned.1.call-done = bf16[4,1,4,2,128,128]{5,4,3,2,1,0:T(8,128)(2,1)} async-done(((bf16[1,1,4,2,128,128]{5,4,3,2,1,0:T(8,128)(2,1)}), bf16[4,1,4,2,128,128]{5,4,3,2,1,0:T(8,128)(2,1)}) %all-gather.2.cloned.1.call-update) | async-done | bytes 1048592 | tf_op jit(solution)/shard_map/all_gather | solution.py:41
  38.0 0.0 copy-done.1
  38.0 2.5 %convolution_convert_fusion = bf16[4,2,4,2,128,128]{5,0,4,3,2,1:T(4,128)(2,1)S(1)} fusion(bf16[4,1,4,2,128,128]{5,4,3,2,1,0:T(8,128)(2,1)} %all-gather.2.cloned.1.call-done, s32[4,2]{0,1:T(2,128)S(1)} %copy-done.1), kind=kOutput, calls=%fused_computation.3 | convolution fusion | flops 9437216 | bytes 3145760 | tf_op jit(solution)/shard_map/csx,jxrab->jcsrab/dot_general | solution.py:43
  40.5 2.2 %convert_bitcast_fusion = bf16[1,4,4,2,256,128]{4,5,1,3,2,0:T(8,128)(2,1)} fusion(bf16[4,4,2,256,128]{4,1,3,0,2:T(4,128)(2,1)S(1)} %bitcast.97, bf16[1,4,2,128,128]{4,3,2,1,0:T(8,128)(2,1)S(1)} %get-tuple-element.15, bf16[1,4,2,128,128]{4,3,2,1,0:T(8,128)(2,1)S(1)} %get-tuple-element.16, bf16[1,4,2,128,128]{4,3,2,1,0:T(8,128)(2,1)S(1)} %fusion.43), kind=kOutput, calls=%fused_computation.2 | convolution fusion | flops 542113792 | bytes 4980736 | tf_op jit(solution)/shard_map/kcsxy,jcsyd->kjcsxd/dot_general | solution.py:51
  42.7 2.5 %reshape.91 = bf16[1,4,4,2,2,128,128]{5,4,6,1,3,2,0:T(2,128)(2,1)S(1)} reshape(bf16[1,4,4,2,256,128]{4,5,1,3,2,0:T(8,128)(2,1)} %convert_bitcast_fusion) | data formatting | bytes 4194304 | tf_op jit(solution)/shard_map/reshape | solution.py:55
  45.3 6.5 %copy.20 = bf16[1,4,4,2,128,2,128]{6,5,4,3,1,2,0:T(2,128)(2,1)} copy(bf16[1,4,4,2,128,2,128]{4,5,6,1,3,2,0:T(2,128)(2,1)S(1)} %bitcast.96) | data formatting | bytes 4194304 | tf_op jit(solution)/shard_map/transpose | solution.py:56
  51.7 3.2 %reshape.92 = bf16[4,4,2,128,256]{4,3,2,0,1:T(8,128)(2,1)S(1)} reshape(bf16[1,4,4,2,128,2,128]{6,5,4,3,1,2,0:T(2,128)(2,1)} %copy.20) | data formatting | bytes 4194304 | tf_op jit(solution)/shard_map/reshape.3
  54.9 2.1 %fusion.8 = f32[4,256,4,128,1]{3,1,4,2,0:T(8,128)} fusion(bf16[4,4,2,128,256]{4,3,2,0,1:T(8,128)(2,1)S(1)} %reshape.92, bf16[1,4,2,128,128]{3,4,2,1,0:T(8,128)(2,1)S(1)} %get-tuple-element.14, bf16[1,4,2,128,128]{3,4,2,1,0:T(8,128)(2,1)S(1)} %get-tuple-element.13, bf16[1,4,2,128,128]{3,4,2,1,0:T(8,128)(2,1)S(1)} %fusion.44), kind=kOutput, calls=%fused_computation.11 | convolution fusion | flops 541065216 | bytes 4980736 | tf_op jit(solution)/shard_map/kjcsay,kcsyz->kjcsaz/dot_general | solution.py:59
  57.0 2.1 %copy.21 = f32[4,4,128,2,128]{4,0,3,2,1:T(4,128)S(1)} copy(f32[4,4,128,2,128]{2,4,3,0,1:T(8,128)} %bitcast.98) | data formatting | bytes 4194304 | tf_op jit(solution)/shard_map/reshape.12
  59.1 0.0 copy-start.2
  59.2 3.8 %convolution_bitcast_fusion = f32[4,4,2,128,128]{4,0,2,3,1:T(4,128)S(1)} fusion(f32[4,4,128,2,128]{4,0,3,2,1:T(4,128)S(1)} %copy.21, f32[4,4,1,1,1]{0,1,4,3,2:T(4,128)S(1)} %convolution_bitcast_fusion.1), kind=kOutput, calls=%fused_computation.8 | convolution fusion | flops 25165824 | bytes 4194368 | tf_op jit(solution)/shard_map/kjn,kjcsare->kncrae/dot_general | solution.py:63
  63.0 0.0 copy-done.2
  63.0 3.9 %fusion.6 = f32[4,4,2,128,128]{4,0,3,2,1:T(4,128)S(1)} fusion(f32[4,4,2,128,128]{4,0,2,3,1:T(4,128)S(1)} %convolution_bitcast_fusion, f32[4]{0:T(128)S(1)} %broadcast_add_fusion, s32[4]{0:T(128)S(1)} %copy-done.2, s32[4]{0:T(128)S(1)} %iota_add_fusion), kind=kOutput, calls=%fused_computation.6 | convolution fusion | flops 25165856 | bytes 4194352 | tf_op jit(solution)/shard_map/dn,kncrab->dkcrab/dot_general | solution.py:66
  66.9 0.0 copy-start.3
  66.9 1.9 %fusion.46 = (f32[1,4,2,128,128]{4,0,3,2,1:T(1,128)S(1)}, f32[1,4,2,128,128]{4,0,3,2,1:T(1,128)S(1)}, f32[1,4,2,128,128]{4,0,3,2,1:T(1,128)S(1)}, f32[1,4,2,128,128]{4,0,3,2,1:T(1,128)S(1)}) fusion(f32[4,4,2,128,128]{4,0,3,2,1:T(4,128)S(1)} %fusion.6), kind=kLoop, calls=%fused_computation.58 | loop fusion | bytes 4194304 | tf_op jit(solution)/shard_map/slice | solution.py:72
  68.8 3.8 %collective-permute-start = (f32[1,4,2,128,128]{4,0,3,2,1:T(1,128)S(1)}, f32[1,4,2,128,128]{4,0,3,2,1:T(1,128)S(1)}, u32[]{:S(2)}, u32[]{:S(2)}) collective-permute-start(f32[1,4,2,128,128]{4,0,3,2,1:T(1,128)S(1)} %get-tuple-element.9), channel_id=1, source_target_pairs={{0,4},{4,8},{8,12},{12,16},{16,20},{20,24},{24,28},{1,5},{5,9},{9,... | collective-permute-start | bytes 1572872 | tf_op jit(solution)/shard_map/ppermute | solution.py:12
  72.6 1.3 collective-permute-start.6
  73.9 2.1 %collective-permute-start.4 = (f32[1,4,2,128,128]{4,0,3,2,1:T(1,128)S(1)}, f32[1,4,2,128,128]{4,0,3,2,1:T(1,128)S(1)}, u32[]{:S(2)}, u32[]{:S(2)}) collective-permute-start(f32[1,4,2,128,128]{4,0,3,2,1:T(1,128)S(1)} %get-tuple-element.11), channel_id=1, source_target_pairs={{0,12},{4,16},{8,20},{12,24},{16,28},{1,13},{5,17},{9,21},{13,25},... | collective-permute-start | bytes 1572872 | tf_op jit(solution)/shard_map/ppermute | solution.py:12
  76.0 0.0 copy-done.3
  76.0 3.9 %fusion.4 = f32[4,4,2,128,128]{4,0,3,2,1:T(4,128)S(1)} fusion(f32[4,4,2,128,128]{4,0,2,3,1:T(4,128)S(1)} %convolution_bitcast_fusion, f32[4]{0:T(128)S(1)} %copy-done.3, s32[4]{0:T(128)S(1)} %copy-done.2, s32[4]{0:T(128)S(1)} %iota_add_fusion), kind=kOutput, calls=%fused_computation.4 | convolution fusion | flops 25165856 | bytes 4194352 | tf_op jit(solution)/shard_map/dn,kncrab->dkcrab/dot_general | solution.py:69
  79.9 2.4 %collective-permute-start.2 = (f32[1,4,2,128,128]{4,0,3,2,1:T(1,128)S(1)}, f32[1,4,2,128,128]{4,0,3,2,1:T(1,128)S(1)}, u32[]{:S(2)}, u32[]{:S(2)}) collective-permute-start(f32[1,4,2,128,128]{4,0,3,2,1:T(1,128)S(1)} %get-tuple-element.12), channel_id=1, source_target_pairs={{0,8},{4,12},{8,16},{12,20},{16,24},{20,28},{1,9},{5,13},{9,17},{1... | collective-permute-start | bytes 1572872 | tf_op jit(solution)/shard_map/ppermute | solution.py:12
  82.4 1.9 %fusion.45 = (f32[1,4,2,128,128]{4,0,3,2,1:T(1,128)S(1)}, f32[1,4,2,128,128]{4,0,3,2,1:T(1,128)S(1)}, f32[1,4,2,128,128]{4,0,3,2,1:T(1,128)S(1)}, f32[1,4,2,128,128]{4,0,3,2,1:T(1,128)S(1)}) fusion(f32[4,4,2,128,128]{4,0,3,2,1:T(4,128)S(1)} %fusion.4), kind=kLoop, calls=%fused_computation.57 | loop fusion | bytes 4194304 | tf_op jit(solution)/shard_map/slice | solution.py:73
  84.3 3.0 %collective-permute-start.1 = (f32[1,4,2,128,128]{4,0,3,2,1:T(1,128)S(1)}, f32[1,4,2,128,128]{4,0,3,2,1:T(1,128)S(1)}, u32[]{:S(2)}, u32[]{:S(2)}) collective-permute-start(f32[1,4,2,128,128]{4,0,3,2,1:T(1,128)S(1)} %get-tuple-element.5), channel_id=1, source_target_pairs={{4,0},{8,4},{12,8},{16,12},{20,16},{24,20},{28,24},{5,1},{9,5},{13... | collective-permute-start | bytes 1572872 | tf_op jit(solution)/shard_map/ppermute | solution.py:12
  87.2 0.0 collective-permute-done
  87.2 1.3 collective-permute-start.7
  88.5 0.0 collective-permute-done.6
  88.5 21.5 %collective-permute-start.5 = (f32[1,4,2,128,128]{4,0,3,2,1:T(1,128)S(1)}, f32[1,4,2,128,128]{4,0,3,2,1:T(1,128)S(1)}, u32[]{:S(2)}, u32[]{:S(2)}) collective-permute-start(f32[1,4,2,128,128]{4,0,3,2,1:T(1,128)S(1)} %get-tuple-element.7), channel_id=1, source_target_pairs={{12,0},{16,4},{20,8},{24,12},{28,16},{13,1},{17,5},{21,9},{25,13},... | collective-permute-start | bytes 1572872 | tf_op jit(solution)/shard_map/ppermute | solution.py:12
  110.1 0.0 collective-permute-done.4
  110.1 5.4 %collective-permute-start.3 = (f32[1,4,2,128,128]{4,0,3,2,1:T(1,128)S(1)}, f32[1,4,2,128,128]{4,0,3,2,1:T(1,128)S(1)}, u32[]{:S(2)}, u32[]{:S(2)}) collective-permute-start(f32[1,4,2,128,128]{4,0,3,2,1:T(1,128)S(1)} %get-tuple-element.8), channel_id=1, source_target_pairs={{8,0},{12,4},{16,8},{20,12},{24,16},{28,20},{9,1},{13,5},{17,9},{2... | collective-permute-start | bytes 1572872 | tf_op jit(solution)/shard_map/ppermute | solution.py:12
  115.5 0.0 collective-permute-done.2
  115.5 0.0 collective-permute-done.1
  115.5 0.0 collective-permute-done.7
  115.5 15.3 %collective-permute-done.5 = f32[1,4,2,128,128]{4,0,3,2,1:T(1,128)S(1)} collective-permute-done((f32[1,4,2,128,128]{4,0,3,2,1:T(1,128)S(1)}, f32[1,4,2,128,128]{4,0,3,2,1:T(1,128)S(1)}, u32[]{:S(2)}, u32[]{:S(2)}) %collective-permute-start.5) | collective-permute-done | bytes 524320 | tf_op jit(solution)/shard_map/ppermute | solution.py:12
  130.9 0.0 collective-permute-done.3
  130.9 1.1 add_add_fusion
  (1 shorter events, 0.0 us)
Async XLA Ops:
  6.5 0.7 copy-start
  6.5 31.5 %copy-start.1 = (s32[4,2]{0,1:T(2,128)S(1)}, s32[4,2]{0,1:T(2,128)}, u32[]{:S(2)}) copy-start(s32[4,2]{0,1:T(2,128)} %param.12) | copy-start | bytes 100
  6.5 31.4 %all-gather.2.cloned.1.call-start = ((), (), s32[]{:S(2)}) async-start(), calls=%async_computation | async-start | bytes 1310720 | tf_op jit(solution)/shard_map/all_gather | solution.py:41
  59.1 3.9 %copy-start.2 = (s32[4]{0:T(128)S(1)}, s32[4]{0:T(128)}, u32[]{:S(2)}) copy-start(s32[4]{0:T(128)} %param.11) | copy-start | bytes 52
  66.9 9.1 %copy-start.3 = (f32[4]{0:T(128)S(1)}, f32[4]{0:T(128)}, u32[]{:S(2)}) copy-start(f32[4]{0:T(128)} %param.10) | copy-start | bytes 52
  68.8 18.4 %collective-permute-start = (f32[1,4,2,128,128]{4,0,3,2,1:T(1,128)S(1)}, f32[1,4,2,128,128]{4,0,3,2,1:T(1,128)S(1)}, u32[]{:S(2)}, u32[]{:S(2)}) collective-permute-start(f32[1,4,2,128,128]{4,0,3,2,1:T(1,128)S(1)} %get-tuple-element.9), channel_id=1, source_target_pairs={{0,4},{4,8},{8,12},{12,16},{16,20},{20,24},{24,28},{1,5},{5,9},{9,... | collective-permute-start | bytes 1572872 | tf_op jit(solution)/shard_map/ppermute | solution.py:12
  72.6 15.9 %collective-permute-start.6 = (f32[1,4,2,128,128]{4,0,3,2,1:T(1,128)S(1)}, f32[1,4,2,128,128]{4,0,3,2,1:T(1,128)S(1)}, u32[]{:S(2)}, u32[]{:S(2)}) collective-permute-start(f32[1,4,2,128,128]{4,0,3,2,1:T(1,128)S(1)} %get-tuple-element.10), channel_id=1, source_target_pairs={{0,16},{4,20},{8,24},{12,28},{1,17},{5,21},{9,25},{13,29},{2,18},{... | collective-permute-start | bytes 1572872 | tf_op jit(solution)/shard_map/ppermute | solution.py:12
  73.9 36.2 %collective-permute-start.4 = (f32[1,4,2,128,128]{4,0,3,2,1:T(1,128)S(1)}, f32[1,4,2,128,128]{4,0,3,2,1:T(1,128)S(1)}, u32[]{:S(2)}, u32[]{:S(2)}) collective-permute-start(f32[1,4,2,128,128]{4,0,3,2,1:T(1,128)S(1)} %get-tuple-element.11), channel_id=1, source_target_pairs={{0,12},{4,16},{8,20},{12,24},{16,28},{1,13},{5,17},{9,21},{13,25},... | collective-permute-start | bytes 1572872 | tf_op jit(solution)/shard_map/ppermute | solution.py:12
  79.9 35.5 %collective-permute-start.2 = (f32[1,4,2,128,128]{4,0,3,2,1:T(1,128)S(1)}, f32[1,4,2,128,128]{4,0,3,2,1:T(1,128)S(1)}, u32[]{:S(2)}, u32[]{:S(2)}) collective-permute-start(f32[1,4,2,128,128]{4,0,3,2,1:T(1,128)S(1)} %get-tuple-element.12), channel_id=1, source_target_pairs={{0,8},{4,12},{8,16},{12,20},{16,24},{20,28},{1,9},{5,13},{9,17},{1... | collective-permute-start | bytes 1572872 | tf_op jit(solution)/shard_map/ppermute | solution.py:12
  84.3 31.3 %collective-permute-start.1 = (f32[1,4,2,128,128]{4,0,3,2,1:T(1,128)S(1)}, f32[1,4,2,128,128]{4,0,3,2,1:T(1,128)S(1)}, u32[]{:S(2)}, u32[]{:S(2)}) collective-permute-start(f32[1,4,2,128,128]{4,0,3,2,1:T(1,128)S(1)} %get-tuple-element.5), channel_id=1, source_target_pairs={{4,0},{8,4},{12,8},{16,12},{20,16},{24,20},{28,24},{5,1},{9,5},{13... | collective-permute-start | bytes 1572872 | tf_op jit(solution)/shard_map/ppermute | solution.py:12
  87.2 28.3 %collective-permute-start.7 = (f32[1,4,2,128,128]{4,0,3,2,1:T(1,128)S(1)}, f32[1,4,2,128,128]{4,0,3,2,1:T(1,128)S(1)}, u32[]{:S(2)}, u32[]{:S(2)}) collective-permute-start(f32[1,4,2,128,128]{4,0,3,2,1:T(1,128)S(1)} %get-tuple-element.6), channel_id=1, source_target_pairs={{16,0},{20,4},{24,8},{28,12},{17,1},{21,5},{25,9},{29,13},{18,2},{... | collective-permute-start | bytes 1572872 | tf_op jit(solution)/shard_map/ppermute | solution.py:12
  88.5 42.3 %collective-permute-start.5 = (f32[1,4,2,128,128]{4,0,3,2,1:T(1,128)S(1)}, f32[1,4,2,128,128]{4,0,3,2,1:T(1,128)S(1)}, u32[]{:S(2)}, u32[]{:S(2)}) collective-permute-start(f32[1,4,2,128,128]{4,0,3,2,1:T(1,128)S(1)} %get-tuple-element.7), channel_id=1, source_target_pairs={{12,0},{16,4},{20,8},{24,12},{28,16},{13,1},{17,5},{21,9},{25,13},... | collective-permute-start | bytes 1572872 | tf_op jit(solution)/shard_map/ppermute | solution.py:12
  110.1 20.8 %collective-permute-start.3 = (f32[1,4,2,128,128]{4,0,3,2,1:T(1,128)S(1)}, f32[1,4,2,128,128]{4,0,3,2,1:T(1,128)S(1)}, u32[]{:S(2)}, u32[]{:S(2)}) collective-permute-start(f32[1,4,2,128,128]{4,0,3,2,1:T(1,128)S(1)} %get-tuple-element.8), channel_id=1, source_target_pairs={{8,0},{12,4},{16,8},{20,12},{24,16},{28,20},{9,1},{13,5},{17,9},{2... | collective-permute-start | bytes 1572872 | tf_op jit(solution)/shard_map/ppermute | solution.py:12
Sparse Core Ops, SparseCore 0:
  8.9 29.0 all-gather.1
where the time goes:
time: 139 us
  waiting for transfers between devices  42 us (30%)
  starting transfers between devices  40.8 us (29%)
  local copies, waits for them, and re-layouts  19.3 us (14%)
  matrix products  19.3 us (14%)
  between operations  13.6 us (10%)
  other arithmetic  3.72 us (3%)
    ppermute x8, starting transfers between devices, passed_along(): lax.ppermute(value, axis, [(source, source + steps) for source in range(i...  40.8 us
    all_gather x1, waiting for transfers between devices, shards(): piece = lax.all_gather(green, 'mom', axis=0, tiled=True)  25.9 us
    ppermute x8, waiting for transfers between devices, passed_along(): lax.ppermute(value, axis, [(source, source + steps) for source in range(i...  15.4 us
    transpose x1, local copies, waits for them, and re-layouts, shards(): jnp.swapaxes(product, 4, 5)  6.48 us
    another operation x2, local copies, waits for them, and re-layouts  5.28 us
    dot_general x1, matrix products, shards(): jnp.einsum('dn,kncrab->dkcrab', select * occupation[None, :], accum, prec...  3.9 us
    dot_general x1, matrix products, shards(): jnp.einsum('dn,kncrab->dkcrab', select * (1.0 + occupation[None, :]), acc...  3.9 us
    dot_general x1, matrix products, shards(): accum = jnp.einsum('kjn,kjcsare->kncrae', weights, triple, precision=high)  3.84 us
  transfers between devices with their start and end apart: 9, of which 2 were waited for; matrix products, arithmetic and copies ran while one was open for 8% of the time, Pallas kernels for 0%

commit v1 on v0

v1 whole, which is shorter than its diff:
```python
import functools

import jax
import jax.numpy as jnp
from jax import lax
from jax.experimental import pallas as pl
from jax.experimental.pallas import tpu as pltpu
from jax.sharding import PartitionSpec as P

MAXOFF = 4
GROUP = 8
ROWS = 16
LANES = 128
MESH = pl.DeviceIdType.MESH


def kernel(
    momenta,
    groups,
    group,
    green,
    grad,
    coupling,
    occupation,
    offsets,
    neighbours,
    qtable,
    out,
    held,
    coeffs,
    mixer,
    mixed,
    summed,
    blocks,
    left,
    right,
    grad_sem,
    send_sem,
    recv_sem,
    low_sem,
    high_sem,
    halo_sem,
    coeff_send,
    coeff_recv,
    back_send,
    back_recv,
):
    halves = held.shape[0]
    parts = momenta * group
    clusters, per = summed.shape[:2]
    listed = blocks.shape[1]
    modes = occupation.shape[0]
    orbits = blocks.shape[3]
    energy = lax.axis_index("energy")
    mom = lax.axis_index("mom")
    team = energy // group
    rank = energy % group
    base = team * group
    mine = mom * group + rank

    grad_copy = pltpu.make_async_copy(grad, blocks, grad_sem)
    grad_copy.start()
    own_copy = pltpu.make_async_copy(
        green.at[mine], held.at[:, rank + MAXOFF, mom], recv_sem
    )
    own_copy.start()

    barrier = pltpu.get_barrier_semaphore()

    def greet(start, first, count):
        def step(index, carry):
            place = lax.rem(mine + index, parts)
            pl.semaphore_signal(
                barrier,
                inc=1,
                device_id=(start + place % group, place // group),
                device_id_type=MESH,
            )
            return carry

        lax.fori_loop(first, count, step, 0)

    greet(base, 1, parts)
    if groups > 1:

        @pl.when(team > 0)
        def _():
            greet(base - group, 0, parts)

        @pl.when(team < groups - 1)
        def _():
            greet(base + group, 0, parts)

    lane = lax.broadcasted_iota(jnp.int32, coeffs.shape[1:], 1) // ROWS
    line = lax.broadcasted_iota(jnp.int32, coeffs.shape[1:], 0)
    spread = line * (LANES // ROWS) + lane
    value = jnp.zeros(coeffs.shape[1:], jnp.float32)
    for side in range(2):
        for step in range(MAXOFF):
            distance = MAXOFF - step if side == 0 else step + 1
            factors = []
            for mode in range(modes):
                factor = occupation[mode] + (1.0 if side == 0 else 0.0)
                factors.append(jnp.where(offsets[mode] == distance, factor, 0.0))
            for j in range(momenta):
                weight = factors[0] * coupling[qtable[0, j], 0]
                for mode in range(1, modes):
                    weight = weight + factors[mode] * coupling[qtable[0, j], mode]
                place = (side * MAXOFF + step) * momenta + j
                value = jnp.where(spread == place, weight, value)
    coeffs[mom] = value

    empty = jnp.zeros((halves, MAXOFF) + held.shape[2:], held.dtype)
    if groups == 1:
        held[:, :MAXOFF] = empty
        held[:, group + MAXOFF :] = empty
    else:

        @pl.when(team == 0)
        def _():
            held[:, :MAXOFF] = empty

        @pl.when(team == groups - 1)
        def _():
            held[:, group + MAXOFF :] = empty

    pl.semaphore_wait(barrier, parts - 1)
    if groups > 1:

        @pl.when(team > 0)
        def _():
            pl.semaphore_wait(barrier, parts)

        @pl.when(team < groups - 1)
        def _():
            pl.semaphore_wait(barrier, parts)

    def coeff_copy(index):
        return pltpu.make_async_remote_copy(
            src_ref=coeffs.at[mom],
            dst_ref=coeffs.at[mom],
            send_sem=coeff_send.at[index],
            recv_sem=coeff_recv.at[index],
            device_id=(energy, lax.rem(mom + index, momenta)),
            device_id_type=MESH,
        )

    for index in range(1, momenta):
        coeff_copy(index).start()

    def spread_out(start, first, slot, sent, received):
        def step(index, carry):
            place = lax.rem(mine + index, parts)
            pltpu.make_async_remote_copy(
                src_ref=green.at[place],
                dst_ref=held.at[:, slot, mom],
                send_sem=sent,
                recv_sem=received,
                device_id=(start + place % group, place // group),
                device_id_type=MESH,
            ).start()
            return carry

        lax.fori_loop(first, parts, step, 0)

    spread_out(base, 1, rank + MAXOFF, send_sem, recv_sem)
    before = (rank < MAXOFF) & (team > 0)
    after = (rank >= group - MAXOFF) & (team < groups - 1)
    if groups > 1:

        @pl.when(before)
        def _():
            spread_out(base - group, 0, rank + group + MAXOFF, halo_sem, high_sem)

        @pl.when(after)
        def _():
            spread_out(base + group, 0, rank + MAXOFF - group, halo_sem, low_sem)

    grad_copy.wait()
    for cluster in range(clusters):
        for place in range(listed):
            real = blocks[cluster, place, 0]
            imag = blocks[cluster, place, 1]
            left[cluster, place, :orbits, :orbits] = real
            left[cluster, place, :orbits, orbits:] = -imag
            left[cluster, place, orbits:, :orbits] = imag
            left[cluster, place, orbits:, orbits:] = real
            right[cluster, place, :orbits, :orbits] = real
            right[cluster, place, :orbits, orbits:] = imag
            right[cluster, place, orbits:, :orbits] = -imag
            right[cluster, place, orbits:, orbits:] = real

    for index in range(1, momenta):
        coeff_copy(index).wait_recv()
    diagonal = lax.broadcasted_iota(jnp.int32, (ROWS, LANES), 0) == (
        lax.broadcasted_iota(jnp.int32, (ROWS, LANES), 1) % ROWS
    )
    per_side = MAXOFF * momenta * ROWS // LANES
    for k in range(momenta):
        for row in range(2 * per_side):
            full = jnp.where(
                diagonal,
                jnp.broadcast_to(coeffs[k, row : row + 1, :], (ROWS, LANES)),
                0.0,
            )
            high = full.astype(jnp.bfloat16)
            low = (full - high.astype(jnp.float32)).astype(jnp.bfloat16)
            side, column = row // per_side, row % per_side
            columns = slice(column * LANES, (column + 1) * LANES)
            mixer[side, k * ROWS : (k + 1) * ROWS, columns] = high
            mixer[side, (momenta + k) * ROWS : (momenta + k + 1) * ROWS, columns] = low

    arrived = held.at[:, pl.ds(MAXOFF, group)]
    pltpu.make_async_copy(arrived, arrived, recv_sem).wait()
    if groups > 1:

        @pl.when(team > 0)
        def _():
            halo = held.at[:, pl.ds(0, MAXOFF)]
            pltpu.make_async_copy(halo, halo, low_sem).wait()

        @pl.when(team < groups - 1)
        def _():
            halo = held.at[:, pl.ds(group + MAXOFF, MAXOFF)]
            pltpu.make_async_copy(halo, halo, high_sem).wait()

    home = summed.at[mine // per, mine % per]

    def mix(index, carry):
        target = lax.rem(rank + 1 + index, group)
        for half in range(halves):
            below = held[half, pl.ds(target, MAXOFF)]
            above = held[half, pl.ds(target + MAXOFF + 1, MAXOFF)]
            total = jnp.dot(
                mixer[0],
                below.reshape(MAXOFF * momenta * ROWS, LANES),
                preferred_element_type=jnp.float32,
            ) + jnp.dot(
                mixer[1],
                above.reshape(MAXOFF * momenta * ROWS, LANES),
                preferred_element_type=jnp.float32,
            )
            total = total[: momenta * ROWS] + total[momenta * ROWS :]
            mixed[target, :, half] = total.astype(jnp.bfloat16).reshape(
                momenta, ROWS, LANES
            )

        def send(k):
            pltpu.make_async_remote_copy(
                src_ref=mixed.at[target, k],
                dst_ref=home,
                send_sem=back_send,
                recv_sem=back_recv,
                device_id=(base + target, k),
                device_id_type=MESH,
            ).start()

        for step in range(1, momenta):
            send(lax.rem(mom + step, momenta))

        @pl.when(target != rank)
        def _():
            send(mom)

        return carry

    lax.fori_loop(0, group, mix, 0)
    pltpu.make_async_copy(mixed.at[rank, mom], home, back_recv).start()
    pltpu.make_async_copy(summed, summed, back_recv).wait()

    for cluster in range(clusters):
        total = None
        for place in range(listed):
            chosen = summed[neighbours[cluster, place]].reshape(2 * orbits, orbits)
            prod = jnp.dot(left[cluster, place], chosen, preferred_element_type=jnp.float32)
            high = prod.astype(jnp.bfloat16)
            low = (prod - high.astype(jnp.float32)).astype(jnp.bfloat16)
            both = jnp.concatenate(
                [
                    jnp.concatenate([high[:orbits], high[orbits:]], axis=1),
                    jnp.concatenate([low[:orbits], low[orbits:]], axis=1),
                ],
                axis=0,
            )
            triple = lax.dot_general(
                both,
                right[cluster, place],
                (((1,), (1,)), ((), ())),
                preferred_element_type=jnp.float32,
            )
            triple = triple[:orbits] + triple[orbits:]
            total = triple if total is None else total + triple
        out[cluster, 0] = total[:, :orbits]
        out[cluster, 1] = total[:, orbits:]

    for index in range(1, momenta):
        coeff_copy(index).wait_send()
    others = green.at[pl.ds(0, parts - 1)]
    pltpu.make_async_copy(others, others, send_sem).wait()
    pltpu.make_async_copy(others, others, back_send).wait()
    if groups > 1:

        @pl.when(before | after)
        def _():
            pltpu.make_async_copy(green, green, halo_sem).wait()


def shards(teams, group, green, grad, coupling, occupation, offsets, neighbours, qtable):
    momenta = coupling.shape[0]
    clusters, listed = neighbours.shape
    orbits = grad.shape[4]
    parts = momenta * group
    halves = clusters * 2 * orbits * orbits // (parts * ROWS * LANES)
    per = parts // clusters
    pieces = green.reshape(parts, halves, ROWS, LANES)
    vmem = pl.BlockSpec(memory_space=pltpu.VMEM)
    smem = pl.BlockSpec(memory_space=pltpu.SMEM)
    anywhere = pl.BlockSpec(memory_space=pl.ANY)
    dma = pltpu.SemaphoreType.DMA
    result = pl.pallas_call(
        functools.partial(kernel, momenta, teams, group),
        out_shape=jax.ShapeDtypeStruct((clusters, 2, orbits, orbits), jnp.float32),
        in_specs=[anywhere, anywhere, smem, smem, smem, smem, smem],
        out_specs=vmem,
        scratch_shapes=[
            pltpu.VMEM((halves, group + 2 * MAXOFF, momenta, ROWS, LANES), jnp.bfloat16),
            pltpu.VMEM((momenta, max(8, momenta), LANES), jnp.float32),
            pltpu.VMEM((2, 2 * momenta * ROWS, MAXOFF * momenta * ROWS), jnp.bfloat16),
            pltpu.VMEM((group, momenta, halves, ROWS, LANES), jnp.bfloat16),
            pltpu.VMEM((clusters, per, halves, ROWS, LANES), jnp.bfloat16),
            pltpu.VMEM(grad.shape[1:], jnp.bfloat16),
            pltpu.VMEM((clusters, listed, 2 * orbits, 2 * orbits), jnp.bfloat16),
            pltpu.VMEM((clusters, listed, 2 * orbits, 2 * orbits), jnp.bfloat16),
            dma,
            dma,
            dma,
            dma,
            dma,
            dma,
            dma((momenta,)),
            dma((momenta,)),
            dma,
            dma,
        ],
        compiler_params=pltpu.CompilerParams(
            collective_id=0, has_side_effects=True, vmem_limit_bytes=32 * 1024 * 1024
        ),
    )(pieces, grad[0], coupling, occupation, offsets, neighbours, qtable)
    return result[None, None]


def solution(mesh):
    count = mesh.shape["energy"]
    group = GROUP if count % GROUP == 0 else count
    in_specs = (
        P("mom", "energy", None, None, None, None),
        P("mom", None, None, None, None, None),
        P(),
        P(),
        P(),
        P(),
        P("mom", None),
    )
    out_specs = P("mom", "energy", None, None, None, None)
    return jax.shard_map(
        functools.partial(shards, count // group, group),
        mesh=mesh,
        in_specs=in_specs,
        out_specs=out_specs,
        check_vma=False,
    )
```

time: 139 us -> 28.2 us (0.20)
  the two profiles are of different devices: /device:TPU:3 before, /device:TPU:0 now
where the time goes in v1:
time: 28.2 us; the launch traced here: 28 us
  Pallas kernels  23.8 us (84%)
  local copies, waits for them, and re-layouts  4.15 us (15%)
    pallas_call x1, Pallas kernels, shards(): pl.pallas_call(functools.partial(kernel, momenta, teams, group), out_shap...  23.8 us
    unnamed x16, local copies, waits for them, and re-layouts  4.15 us

profile of v1, /device:TPU:0, one launch (start us, length us, event | category | flops | bytes accessed | tf_op | source)
XLA Modules:
  0.0 28.0 jit_solution(14779161559186274122)
XLA Ops:
  0.0 0.0 copy-start.6
  0.0 0.0 copy-start.2
  0.0 0.7 %copy-done.6 = s32[4,2]{0,1:T(2,128)S(1)} copy-done((s32[4,2]{0,1:T(2,128)S(1)}, s32[4,2]{0,1:T(2,128)}, u32[]{:S(2)}) %copy-start.6) | copy-done | bytes 56
  0.7 0.0 copy-start.3
  0.7 0.0 copy-start.4
  0.7 0.0 copy-start.5
  0.7 0.1 copy.8.neighbours
  0.8 0.0 copy-done.2
  0.8 0.6 %copy-done.3 = f32[4]{0:T(128)S(1)} copy-done((f32[4]{0:T(128)S(1)}, f32[4]{0:T(128)}, u32[]{:S(2)}) %copy-start.3) | copy-done | bytes 40
  1.3 0.0 copy-done.4
  1.4 0.0 copy-done.5
  1.4 0.0 copy-start
  1.4 1.0 %copy-done = bf16[1,4,2,2,128,128]{5,4,3,2,1,0:T(8,128)(2,1)S(1)} copy-done((bf16[1,4,2,2,128,128]{5,4,3,2,1,0:T(8,128)(2,1)S(1)}, bf16[1,4,2,2,128,128]{5,4,3,2,1,0:T(8,128)(2,1)}, u32[]{:S(2)}) %copy-start) | copy-done | bytes 524312
  2.4 0.0 copy-start.1
  2.4 0.9 %copy-done.1 = bf16[1,1,4,2,128,128]{5,4,3,2,1,0:T(8,128)(2,1)S(1)} copy-done((bf16[1,1,4,2,128,128]{5,4,3,2,1,0:T(8,128)(2,1)S(1)}, bf16[1,1,4,2,128,128]{5,4,3,2,1,0:T(8,128)(2,1)}, u32[]{:S(2)}) %copy-start.1) | copy-done | bytes 262168
  3.4 23.8 %shard_map.73 = f32[4,2,128,128]{3,2,1,0:T(8,128)S(1)} custom-call(bf16[32,2,16,128]{3,2,1,0:T(8,128)(2,1)S(1)} %bitcast.5, bf16[4,2,2,128,128]{4,3,2,1,0:T(8,128)(2,1)S(1)} %bitcast.4, f32[4,4]{1,0:T(4,128)S(1)} %copy-done.2, f32[4]{0:T(128)S(1)} %copy-done.3, s32[4]{0:T(128)S(1)} %copy-done.4, s32[4,2]{1,0:T(4,128)S(1)} %copy.8.neighbours, ...), custom_call_target="tpu_custom_call" | custom-call | tf_op jit(solution)/shard_map/pallas_call | solution.py:320
  27.2 0.8 %copy.10 = f32[1,1,4,2,128,128]{5,4,3,2,1,0:T(8,128)} copy(f32[1,1,4,2,128,128]{5,4,3,2,1,0:T(8,128)S(1)} %bitcast.3) | data formatting | bytes 1048576
Async XLA Ops:
  0.0 0.7 %copy-start.6 = (s32[4,2]{0,1:T(2,128)S(1)}, s32[4,2]{0,1:T(2,128)}, u32[]{:S(2)}) copy-start(s32[4,2]{0,1:T(2,128)} %param.12) | copy-start | bytes 100
  0.0 0.8 %copy-start.2 = (f32[4,4]{1,0:T(4,128)S(1)}, f32[4,4]{1,0:T(4,128)}, u32[]{:S(2)}) copy-start(f32[4,4]{1,0:T(4,128)} %coupling.1) | copy-start | bytes 196
  0.7 0.7 %copy-start.3 = (f32[4]{0:T(128)S(1)}, f32[4]{0:T(128)}, u32[]{:S(2)}) copy-start(f32[4]{0:T(128)} %occupation.1) | copy-start | bytes 52
  0.7 0.7 %copy-start.4 = (s32[4]{0:T(128)S(1)}, s32[4]{0:T(128)}, u32[]{:S(2)}) copy-start(s32[4]{0:T(128)} %offsets.1) | copy-start | bytes 52
  0.7 0.7 %copy-start.5 = (s32[1,4]{1,0:T(1,128)S(1)}, s32[1,4]{1,0:T(1,128)}, u32[]{:S(2)}) copy-start(s32[1,4]{1,0:T(1,128)} %qtable.1) | copy-start | bytes 52
  1.4 1.0 %copy-start = (bf16[1,4,2,2,128,128]{5,4,3,2,1,0:T(8,128)(2,1)S(1)}, bf16[1,4,2,2,128,128]{5,4,3,2,1,0:T(8,128)(2,1)}, u32[]{:S(2)}) copy-start(bf16[1,4,2,2,128,128]{5,4,3,2,1,0:T(8,128)(2,1)} %param.8) | copy-start | bytes 1572868
  2.4 0.9 %copy-start.1 = (bf16[1,1,4,2,128,128]{5,4,3,2,1,0:T(8,128)(2,1)S(1)}, bf16[1,1,4,2,128,128]{5,4,3,2,1,0:T(8,128)(2,1)}, u32[]{:S(2)}) copy-start(bf16[1,1,4,2,128,128]{5,4,3,2,1,0:T(8,128)(2,1)} %param.7) | copy-start | bytes 786436

commit v2 on v1

--- a/solution.py
+++ b/solution.py
@@ -20,11 +20,11 @@
     group,
     green,
     grad,
-    coupling,
-    occupation,
-    offsets,
-    neighbours,
-    qtable,
+    coupling_hbm,
+    occupation_hbm,
+    offsets_hbm,
+    neighbours_hbm,
+    qtable_hbm,
     out,
     held,
     coeffs,
@@ -34,6 +34,12 @@
     blocks,
     left,
     right,
+    coupling,
+    occupation,
+    offsets,
+    neighbours,
+    qtable,
+    small_sem,
     grad_sem,
     send_sem,
     recv_sem,
@@ -58,6 +64,20 @@
     base = team * group
     mine = mom * group + rank
 
+    small_copies = [
+        pltpu.make_async_copy(source, target, small_sem.at[index])
+        for index, (source, target) in enumerate(
+            [
+                (coupling_hbm, coupling),
+                (occupation_hbm, occupation),
+                (offsets_hbm, offsets),
+                (qtable_hbm, qtable),
+                (neighbours_hbm, neighbours),
+            ]
+        )
+    ]
+    for copy in small_copies:
+        copy.start()
     grad_copy = pltpu.make_async_copy(grad, blocks, grad_sem)
     grad_copy.start()
     own_copy = pltpu.make_async_copy(
@@ -91,6 +111,8 @@
         def _():
             greet(base + group, 0, parts)
 
+    for copy in small_copies:
+        copy.wait()
     lane = lax.broadcasted_iota(jnp.int32, coeffs.shape[1:], 1) // ROWS
     line = lax.broadcasted_iota(jnp.int32, coeffs.shape[1:], 0)
     spread = line * (LANES // ROWS) + lane
@@ -271,7 +293,7 @@
     for cluster in range(clusters):
         total = None
         for place in range(listed):
-            chosen = summed[neighbours[cluster, place]].reshape(2 * orbits, orbits)
+            chosen = summed[neighbours[place, cluster]].reshape(2 * orbits, orbits)
             prod = jnp.dot(left[cluster, place], chosen, preferred_element_type=jnp.float32)
             high = prod.astype(jnp.bfloat16)
             low = (prod - high.astype(jnp.float32)).astype(jnp.bfloat16)
@@ -314,13 +336,12 @@
     per = parts // clusters
     pieces = green.reshape(parts, halves, ROWS, LANES)
     vmem = pl.BlockSpec(memory_space=pltpu.VMEM)
-    smem = pl.BlockSpec(memory_space=pltpu.SMEM)
     anywhere = pl.BlockSpec(memory_space=pl.ANY)
     dma = pltpu.SemaphoreType.DMA
     result = pl.pallas_call(
         functools.partial(kernel, momenta, teams, group),
         out_shape=jax.ShapeDtypeStruct((clusters, 2, orbits, orbits), jnp.float32),
-        in_specs=[anywhere, anywhere, smem, smem, smem, smem, smem],
+        in_specs=[anywhere] * 7,
         out_specs=vmem,
         scratch_shapes=[
             pltpu.VMEM((halves, group + 2 * MAXOFF, momenta, ROWS, LANES), jnp.bfloat16),
@@ -331,6 +352,12 @@
             pltpu.VMEM(grad.shape[1:], jnp.bfloat16),
             pltpu.VMEM((clusters, listed, 2 * orbits, 2 * orbits), jnp.bfloat16),
             pltpu.VMEM((clusters, listed, 2 * orbits, 2 * orbits), jnp.bfloat16),
+            pltpu.SMEM(coupling.shape, jnp.float32),
+            pltpu.SMEM(occupation.shape, jnp.float32),
+            pltpu.SMEM(offsets.shape, jnp.int32),
+            pltpu.SMEM(neighbours.shape[::-1], jnp.int32),
+            pltpu.SMEM(qtable.shape, jnp.int32),
+            dma((5,)),
             dma,
             dma,
             dma,
@@ -343,9 +370,9 @@
             dma,
         ],
         compiler_params=pltpu.CompilerParams(
-            collective_id=0, has_side_effects=True, vmem_limit_bytes=32 * 1024 * 1024
+            collective_id=0, has_side_effects=True, vmem_limit_bytes=60 * 1024 * 1024
         ),
-    )(pieces, grad[0], coupling, occupation, offsets, neighbours, qtable)
+    )(pieces, grad[0], coupling, occupation, offsets, neighbours.T, qtable)
     return result[None, None]
 
 

time: 28.2 us -> 26 us (0.922)
  local copies, waits for them, and re-layouts: 4.15 us -> 1.87 us
    unnamed x16 -> x1, local copies, waits for them, and re-layouts: 4.15 us -> 1.87 us
where the time goes in v2:
time: 26 us; the launch traced here: 25.9 us
  Pallas kernels  24 us (92%)
  local copies, waits for them, and re-layouts  1.87 us (7%)
    pallas_call x1, Pallas kernels, shards(): pl.pallas_call(functools.partial(kernel, momenta, teams, group), out_shap...  24 us
    unnamed x1, local copies, waits for them, and re-layouts  1.87 us

profile of v2, /device:TPU:0, one launch (start us, length us, event | category | flops | bytes accessed | tf_op | source)
XLA Modules:
  0.0 25.9 jit_solution(6093887892422354954)
XLA Ops:
  0.0 24.0 %shard_map.73 = f32[4,2,128,128]{3,2,1,0:T(8,128)} custom-call(bf16[32,2,16,128]{3,2,1,0:T(8,128)(2,1)} %bitcast.6, bf16[4,2,2,128,128]{4,3,2,1,0:T(8,128)(2,1)} %bitcast.5, f32[4,4]{1,0:T(4,128)} %coupling_hbm.1, f32[4]{0:T(128)} %occupation_hbm.1, s32[4]{0:T(128)} %offsets_hbm.1, s32[2,4]{1,0:T(2,128)} %bitcast.7, s32[1,4]{1,0:T(1,128)} %qtable_hbm.1), custom_call_target="tpu_custom_call" | custom-call | tf_op jit(solution)/shard_map/pallas_call | solution.py:341
  24.0 1.9 %copy.9 = f32[1,1,4,2,128,128]{5,4,3,2,1,0:T(8,128)} copy(f32[1,1,4,2,128,128]{5,4,3,2,1,0:T(8,128)} %bitcast.4) | data formatting | bytes 1048576

commit v3 on v2

--- a/solution.py
+++ b/solution.py
@@ -340,7 +340,7 @@
     dma = pltpu.SemaphoreType.DMA
     result = pl.pallas_call(
         functools.partial(kernel, momenta, teams, group),
-        out_shape=jax.ShapeDtypeStruct((clusters, 2, orbits, orbits), jnp.float32),
+        out_shape=pltpu.VMEM((clusters, 2, orbits, orbits), jnp.float32),
         in_specs=[anywhere] * 7,
         out_specs=vmem,
         scratch_shapes=[

time: 26 us -> 24.1 us (0.927)
  local copies, waits for them, and re-layouts: 1.87 us -> 0.8 us
  Pallas kernels: 24 us -> 23.2 us
    unnamed x1, local copies, waits for them, and re-layouts: 1.87 us -> 0.8 us
    pallas_call x1, Pallas kernels: 24 us -> 23.2 us  [shards(): pl.pallas_call(functools.partial(kernel, momenta, teams, group), out_shap...]
where the time goes in v3:
time: 24.1 us; the launch traced here: 24 us
  Pallas kernels  23.2 us (96%)
  local copies, waits for them, and re-layouts  0.8 us (3%)
    pallas_call x1, Pallas kernels, shards(): pl.pallas_call(functools.partial(kernel, momenta, teams, group), out_shap...  23.2 us
    unnamed x1, local copies, waits for them, and re-layouts  0.8 us

profile of v3, /device:TPU:0, one launch (start us, length us, event | category | flops | bytes accessed | tf_op | source)
XLA Modules:
  0.0 24.0 jit_solution(1180329104461258282)
XLA Ops:
  0.0 23.2 %shard_map.73 = f32[4,2,128,128]{3,2,1,0:T(8,128)S(1)} custom-call(bf16[32,2,16,128]{3,2,1,0:T(8,128)(2,1)} %bitcast.6, bf16[4,2,2,128,128]{4,3,2,1,0:T(8,128)(2,1)} %bitcast.5, f32[4,4]{1,0:T(4,128)} %coupling_hbm.1, f32[4]{0:T(128)} %occupation_hbm.1, s32[4]{0:T(128)} %offsets_hbm.1, s32[2,4]{1,0:T(2,128)} %bitcast.7, s32[1,4]{1,0:T(1,128)} %qtable_hbm.1), custom_call_target="tpu_custom_call" | custom-call | tf_op jit(solution)/shard_map/pallas_call | solution.py:341
  23.2 0.8 %copy.9 = f32[1,1,4,2,128,128]{5,4,3,2,1,0:T(8,128)} copy(f32[1,1,4,2,128,128]{5,4,3,2,1,0:T(8,128)S(1)} %bitcast.4) | data formatting | bytes 1048576
